TPU v7x, 32 devices: a whole 2x2x4 slice. The times are simulated.
32 devices in a mesh: groups: 2 (over y), shard: 4 (over z), inner: 4 (over x, core).
Axes of the slice: x: 2, y: 2, z: 4, core: 2. Of those that a mesh axis runs over, the one named last changes fastest.
Arguments:
- item_last: bfloat16 [256, 2048], P(('groups', 'shard')), parts along dimension 0, may hold values from -260 to 260, as said below
- adapter: bfloat16 [2048, 4096], P(None, 'inner'), may hold values from -0.125 to 0.125
- user_gain: float32 [4096], replicated, may hold values from 0.5 to 1.5
- w_gate: bfloat16 [4096, 6144], P('shard', 'inner'), may hold values from -0.09375 to 0.09375
- w_up: bfloat16 [4096, 6144], P('shard', 'inner'), may hold values from -0.09375 to 0.09375
- owners: int32 [1024, 1], P(('groups', 'shard')), parts along dimension 0, may hold values from 0 to 3; in each aligned block of 128 rows (0 to 127, 128 to 255, ...) at most 64 rows name the same one
- item_rows: int32 [1024], P(('groups', 'shard')), parts along dimension 0, may hold values from 0 to 31
- lengths: int32 [8], P(('groups', 'shard')), parts along dimension 0, may hold values from 32 to 128
- d_hidden: bfloat16 [1024, 6144], P(('groups', 'shard'), 'inner'), parts along dimension 0, may hold values from -6 to 6
Outputs:
- hidden: bfloat16 [1024, 6144], P(('groups', 'shard'), 'inner'), parts along dimension 0
- item_grad: float32 [256, 4096], P(('groups', 'shard'), 'inner'), parts along dimension 0
There are 2 independent parts, one for each index of `groups`. A program takes and returns all parts, laid end to end along the dimension named above; an argument that names none is the same for every part. Nothing has to cross between parts.
Inputs may be any that keep to these rules, and one draw needn't show every extreme that they name: `owners`: among the rows of one device, no owner is named by more than 64 slots. `item_last`: hidden states of the items' final tokens.
All inputs are finite; a program needn't handle non-finite values.
Results may differ from a plain program's by a relative error of at most 0.012.
Values may be sent and summed in bfloat16 or wider, within the bound.
A program may use at most 128 MiB of HBM per device.

v0:
```python
import jax
import jax.numpy as jnp
from jax import lax
from jax.sharding import PartitionSpec as P

HIST_LEN = 128


epsilon = 1e-05


def contract_rows(left_side, right_side):
    return lax.dot_general(
        left_side, right_side, (((1,), (1,)), ((), ())), preferred_element_type=jnp.float32
    )


def body(item_last, adapter, user_gain, w_gate, w_up, owners, item_rows, lengths, d_hidden):
    shards = lax.axis_size("shard")
    inner_count = lax.axis_size("inner")
    item_count = item_last.shape[0]
    row_count = owners.shape[0]
    model_width = user_gain.shape[0]
    own_width = model_width // inner_count
    capacity = max(2, 2 * row_count // shards)
    embedded = jnp.dot(item_last, adapter, preferred_element_type=jnp.float32).astype(jnp.bfloat16)
    owner_of = owners[:, 0]
    onehot = (owner_of[:, None] == jnp.arange(shards, dtype=jnp.int32)[None, :]).astype(jnp.int32)
    before = jnp.cumsum(onehot, axis=0) - onehot
    slot_of = jnp.sum(before * onehot, axis=1)
    target = owner_of * capacity + slot_of
    requested = jnp.zeros((shards * capacity,), jnp.int32).at[target].set(item_rows)
    requested = requested.reshape(shards, capacity)
    position = jnp.arange(row_count, dtype=jnp.int32) % HIST_LEN
    limit_of = jnp.repeat(lengths, HIST_LEN, total_repeat_length=row_count)
    live_rows = position < limit_of
    whole_table = lax.all_gather(embedded, "shard", axis=0, tiled=True)
    fetched = whole_table[owner_of * item_count + item_rows]
    routed_own = jnp.where(live_rows[:, None], fetched, jnp.zeros_like(fetched))
    routed = lax.all_gather(routed_own, "inner", axis=1, tiled=True)
    routed_f = routed.astype(jnp.float32)
    inv_rms = lax.rsqrt(jnp.mean(routed_f * routed_f, axis=1) + epsilon)
    normed = (routed_f * inv_rms[:, None] * user_gain[None, :]).astype(jnp.bfloat16)
    gate_whole, up_whole = (
        lax.all_gather(w_gate, "shard", axis=0, tiled=True),
        lax.all_gather(w_up, "shard", axis=0, tiled=True),
    )
    gate_act = jnp.dot(normed, gate_whole, preferred_element_type=jnp.float32)
    up_act = jnp.dot(normed, up_whole, preferred_element_type=jnp.float32)
    sigmoid_gate = jax.nn.sigmoid(gate_act)
    active = gate_act * sigmoid_gate
    hidden = (active * up_act).astype(jnp.bfloat16)
    grad_f = d_hidden.astype(jnp.float32)
    d_gate = (grad_f * up_act * sigmoid_gate * (1.0 + gate_act * (1.0 - sigmoid_gate))).astype(
        jnp.bfloat16
    )
    d_up = (grad_f * active).astype(jnp.bfloat16)
    partial_value = contract_rows(d_gate, gate_whole) + contract_rows(d_up, up_whole)
    own_start = lax.axis_index("inner") * own_width
    gain_own = lax.dynamic_slice_in_dim(user_gain, own_start, own_width, 0)
    routed_own_f = routed_own.astype(jnp.float32)
    d_normed_all = lax.psum(partial_value.astype(jnp.bfloat16), "inner").astype(jnp.float32)
    products = jnp.sum(user_gain[None, :] * d_normed_all * routed_f, axis=1)
    d_normed = lax.dynamic_slice_in_dim(d_normed_all, own_start, own_width, 1)
    cubed_scale = inv_rms * inv_rms * inv_rms * products / model_width
    d_routed = inv_rms[:, None] * gain_own[None, :] * d_normed - routed_own_f * cubed_scale[:, None]
    d_routed = jnp.where(live_rows[:, None], d_routed, jnp.zeros_like(d_routed)).astype(
        jnp.bfloat16
    )
    outgoing = jnp.zeros((shards * capacity, own_width), jnp.bfloat16).at[target].set(d_routed)
    outgoing = outgoing.reshape(shards, capacity, own_width)
    arrived_rows, arrived_grads = (
        lax.all_to_all(requested, "shard", split_axis=0, concat_axis=0, tiled=True),
        lax.all_to_all(outgoing, "shard", split_axis=0, concat_axis=0, tiled=True),
    )
    selector = (
        arrived_rows.reshape(1, -1) == jnp.arange(item_count, dtype=jnp.int32)[:, None]
    ).astype(jnp.bfloat16)
    item_grad = jnp.dot(
        selector, arrived_grads.reshape(-1, own_width), preferred_element_type=jnp.float32
    )
    return (hidden, item_grad)


def solution(mesh):
    return jax.shard_map(
        body,
        mesh=mesh,
        in_specs=(
            P(("groups", "shard"), None),
            P(None, "inner"),
            P(),
            P("shard", "inner"),
            P("shard", "inner"),
            P(("groups", "shard"), None),
            P(("groups", "shard")),
            P(("groups", "shard")),
            P(("groups", "shard"), "inner"),
        ),
        out_specs=(P(("groups", "shard"), "inner"), P(("groups", "shard"), "inner")),
        check_vma=False,
    )
```

profile of v0, /device:TPU:0, one launch (start us, length us, event | category | flops | bytes accessed | tf_op | source)
XLA Modules:
  0.0 576.4 jit_solution(14656227141377980324)
XLA Ops:
  7.2 0.8 copy-done
  8.1 3.0 convolution_convert_fusion
  11.1 15.6 %all_gather.12 = bf16[128,1024]{1,0:T(8,128)(2,1)S(1)} all-gather(bf16[32,1024]{1,0:T(8,128)(2,1)S(1)} %convolution_convert_fusion), channel_id=1, replica_groups=mesh['groups'=2,'shard'=4,'inner'=4] {'shard'}, dimensions={0}, use_global_device_ids=true | all-gather | bytes 327680 | tf_op jit(solution)/shard_map/all_gather | solution.py:37
  27.4 0.9 gather_fusion
  28.3 0.8 broadcast_select_fusion
  29.1 0.7 all-gather.6.cloned.1.call-update
  30.6 16.9 %all-gather.4.cloned.1.call-done = bf16[128,4096]{1,0:T(8,128)(2,1)} async-done(((bf16[128,1024]{1,0:T(8,128)(2,1)}), bf16[128,4096]{1,0:T(8,128)(2,1)}) %all-gather.4.cloned.1.call-update) | async-done | bytes 1048592 | tf_op jit(solution)/shard_map/all_gather | solution.py:40
  47.5 1.5 fusion.1
  49.0 218.3 %all-gather.6.cloned.1.call-done = bf16[4096,1536]{1,0:T(8,128)(2,1)} async-done(((bf16[1024,1536]{1,0:T(8,128)(2,1)}), bf16[4096,1536]{1,0:T(8,128)(2,1)}) %all-gather.6.cloned.1.call-update) | async-done | bytes 12582928 | tf_op jit(solution)/shard_map/all_gather | solution.py:45
  267.3 6.8 %fusion.16 = f32[128,1536]{1,0:T(8,128)S(1)} fusion(bf16[4096,1536]{1,0:T(8,128)(2,1)} %all-gather.6.cloned.1.call-done, bf16[128,4096]{1,0:T(8,128)(2,1)} %all-gather.4.cloned.1.call-done, f32[4096]{0:T(1024)S(1)} %copy-done.6, f32[128]{0:T(128)S(1)} %add_rsqrt_fusion), kind=kOutput, calls=%fused_computation.26 | convolution fusion | flops 1612709888 | bytes 14434816 | tf_op jit(solution)/shard_map/dot_general | solution.py:48
  274.1 211.2 %all-gather.8.cloned.1.call-done = bf16[4096,1536]{1,0:T(8,128)(2,1)} async-done(((bf16[1024,1536]{1,0:T(8,128)(2,1)}), bf16[4096,1536]{1,0:T(8,128)(2,1)}) %all-gather.8.cloned.1.call-update) | async-done | bytes 12582928 | tf_op jit(solution)/shard_map/all_gather | solution.py:46
  485.3 7.7 %multiply_convert_fusion = (bf16[128,1536]{1,0:T(8,128)(2,1)}, f32[128,1536]{1,0:T(8,128)}) fusion(f32[128,1536]{1,0:T(8,128)S(1)} %fusion.16, bf16[4096,1536]{1,0:T(8,128)(2,1)} %all-gather.8.cloned.1.call-done, bf16[128,4096]{1,0:T(8,128)(2,1)S(1)} %copy-done.2, f32[4096]{0:T(1024)S(1)} %copy-done.6, f32[128]{0:T(128)S(1)} %add_rsqrt_fusion), kind=kOutput, calls=%fused_computation.19 | convolution fusion | flops 1613889536 | bytes 15614464 | tf_op jit(solution)/shard_map/dot_general | solution.py:49
  493.0 0.9 copy-done.1
  493.9 6.7 %fusion.11 = f32[128,4096]{1,0:T(8,128)} fusion(bf16[4096,1536]{1,0:T(8,128)(2,1)S(1)} %copy-done.1, f32[128,1536]{1,0:T(8,128)} %get-tuple-element.27, bf16[128,1536]{1,0:T(8,128)(2,1)} %param.21, f32[128,1536]{1,0:T(8,128)S(1)} %fusion.16), kind=kOutput, calls=%fused_computation.23 | convolution fusion | flops 1612775424 | bytes 16646144 | tf_op jit(solution)/shard_map/dot_general | solution.py:13
  500.6 10.5 %fusion = bf16[128,4096]{1,0:T(8,128)(2,1)} fusion(f32[128,4096]{1,0:T(8,128)} %fusion.11, bf16[4096,1536]{1,0:T(8,128)(2,1)} %all-gather.8.cloned.1.call-done, bf16[128,1536]{1,0:T(8,128)(2,1)} %param.21, f32[128,1536]{1,0:T(8,128)S(1)} %fusion.16), kind=kOutput, calls=%fused_computation.4 | convolution fusion | flops 1613037568 | bytes 16908288 | tf_op jit(solution)/shard_map/dot_general | solution.py:13
  511.5 1.0 scatter_custom_fusion
  513.1 3.2 all-to-all-start
  516.4 29.2 %all-reduce.2.cloned.1.call-done = bf16[128,4096]{1,0:T(8,128)(2,1)} async-done(((bf16[128,4096]{1,0:T(8,128)(2,1)}), bf16[128,4096]{1,0:T(8,128)(2,1)}) %all-reduce.2.cloned.1.call-update) | async-done | bytes 1048592 | tf_op jit(solution)/shard_map/psum | solution.py:62
  545.6 1.7 fusion.4
  547.6 0.7 copy-done.5
  548.3 2.1 scatter_custom_fusion.1
  550.4 4.6 all-to-all-start.1
  556.2 12.8 %all-to-all-done.1 = bf16[4,64,1024]{2,1,0:T(8,128)(2,1)S(1)} async-done(((bf16[4,64,1024]{2,1,0:T(8,128)(2,1)}), bf16[4,64,1024]{2,1,0:T(8,128)(2,1)S(1)}, u32[]{:S(2)}, u32[]{:S(2)}) %all-to-all-start.1) | async-done | bytes 524320 | tf_op jit(solution)/shard_map/all_to_all | solution.py:74
  569.0 0.8 fusion.27
  (39 shorter events, 3.5 us)
Async XLA Ops:
  7.2 0.9 copy-start
  7.2 19.5 %copy-start.7 = (s32[128,1]{0,1:T(1,128)S(1)}, s32[128,1]{0,1:T(1,128)}, u32[]{:S(2)}) copy-start(s32[128,1]{0,1:T(1,128)} %param.18) | copy-start | bytes 1540
  7.2 19.5 %copy-start.8 = (s32[128]{0:T(128)S(1)}, s32[128]{0:T(128)}, u32[]{:S(2)}) copy-start(s32[128]{0:T(128)} %param.19) | copy-start | bytes 1540
  7.2 40.3 %all-gather.4.cloned.1.call-start = ((), (), s32[]{:S(2)}) async-start(), calls=%async_computation.2 | async-start | bytes 1310720 | tf_op jit(solution)/shard_map/all_gather | solution.py:40
  28.3 2.3 copy-start.4
  29.1 238.2 %all-gather.6.cloned.1.call-start = ((), (), s32[]{:S(2)}) async-start(), calls=%async_computation.3 | async-start | bytes 15728640 | tf_op jit(solution)/shard_map/all_gather | solution.py:45
  29.8 237.5 %copy-start.6 = (f32[4096]{0:T(1024)S(1)}, f32[4096]{0:T(1024)}, u32[]{:S(2)}) copy-start(f32[4096]{0:T(1024)} %param.15) | copy-start | bytes 49156
  29.9 455.5 %all-gather.8.cloned.1.call-start = ((), (), s32[]{:S(2)}) async-start(), calls=%async_computation.4 | async-start | bytes 15728640 | tf_op jit(solution)/shard_map/all_gather | solution.py:46
  30.6 515.0 %all-reduce.2.cloned.1.call-start = ((), (), s32[]{:S(2)}) async-start(), calls=%async_computation.5 | async-start | bytes 2097152 | tf_op jit(solution)/shard_map/psum | solution.py:62
  49.0 436.3 %copy-start.2 = (bf16[128,4096]{1,0:T(8,128)(2,1)S(1)}, bf16[128,4096]{1,0:T(8,128)(2,1)}, u32[]{:S(2)}) copy-start(bf16[128,4096]{1,0:T(8,128)(2,1)} %all-gather.4.cloned.1.call-done) | copy-start | bytes 3145732
  485.3 8.6 %copy-start.1 = (bf16[4096,1536]{1,0:T(8,128)(2,1)S(1)}, bf16[4096,1536]{1,0:T(8,128)(2,1)}, u32[]{:S(2)}) copy-start(bf16[4096,1536]{1,0:T(8,128)(2,1)} %all-gather.6.cloned.1.call-done) | copy-start | bytes 37748740
  513.1 37.2 %all-to-all-start = ((s32[4,1,64]{2,1,0:T(1,128)}), s32[4,1,64]{2,1,0:T(1,128)S(1)}, u32[]{:S(2)}, u32[]{:S(2)}) async-start(s32[4,1,64]{2,1,0:T(1,128)} %all_to_all.9), calls=%async_computation | async-start | bytes 4096 | tf_op jit(solution)/shard_map/all_to_all | solution.py:73
  545.6 1.8 copy-start.3
  547.3 1.0 copy-start.5
  547.3 1.0 dynamic-slice-start
  550.4 18.6 %all-to-all-start.1 = ((bf16[4,64,1024]{2,1,0:T(8,128)(2,1)}), bf16[4,64,1024]{2,1,0:T(8,128)(2,1)S(1)}, u32[]{:S(2)}, u32[]{:S(2)}) async-start(bf16[4,64,1024]{2,1,0:T(8,128)(2,1)} %bitcast.4), calls=%async_computation.1 | async-start | bytes 1048576 | tf_op jit(solution)/shard_map/all_to_all | solution.py:74
Sparse Core Ops, SparseCore 0:
  29.2 18.2 all-gather.3
  49.1 218.2 all-gather.5
  268.9 216.3 all-gather.7
  511.2 34.3 all-reduce.1
where the time goes:
time: 577 us; the launch traced here: 576 us
  waiting for transfers between devices  490 us (85%)
  matrix products  35.4 us (6%)
  blocking collectives  15.6 us (3%)
  between operations  14.6 us (3%)
  starting transfers between devices  7.98 us (1%)
  other arithmetic  7.49 us (1%)
    all_gather x1, waiting for transfers between devices, body(): lax.all_gather(w_gate, 'shard', axis=0, tiled=True)  218 us
    all_gather x1, waiting for transfers between devices, body(): lax.all_gather(w_up, 'shard', axis=0, tiled=True)  211 us
    psum x1, waiting for transfers between devices, body(): lax.psum(partial_value.astype(jnp.bfloat16), 'inner').astype(jnp.float32)  29.2 us
    dot_general x2, matrix products, contract_rows(): lax.dot_general(left_side, right_side, (((1,), (1,)), ((), ())), preferre...  17.1 us
    all_gather x1, waiting for transfers between devices, body(): routed = lax.all_gather(routed_own, 'inner', axis=1, tiled=True)  16.9 us
    all_gather x1, blocking collectives, body(): whole_table = lax.all_gather(embedded, 'shard', axis=0, tiled=True)  15.6 us
    all_to_all x1, waiting for transfers between devices, body(): lax.all_to_all(outgoing, 'shard', split_axis=0, concat_axis=0, tiled=True)  12.8 us
  transfers between devices with their start and end apart: 6, of which 5 were waited for; matrix products, arithmetic and copies ran while one was open for 3% of the time, Pallas kernels for 0%

commit v1 on v0

v1 whole, which is shorter than its diff:
```python
import jax
import jax.numpy as jnp
from jax import lax
from jax.sharding import PartitionSpec as P

HIST_LEN = 128


epsilon = 1e-05


def contract_rows(left_side, right_side):
    return lax.dot_general(
        left_side, right_side, (((1,), (1,)), ((), ())), preferred_element_type=jnp.float32
    )


def body(item_last, adapter, user_gain, w_gate, w_up, owners, item_rows, lengths, d_hidden):
    shards = lax.axis_size("shard")
    inner_count = lax.axis_size("inner")
    own_items = item_last.shape[0]
    items = own_items * shards
    row_count = owners.shape[0]
    model_width = user_gain.shape[0]
    own_width = model_width // inner_count
    weight_rows = w_gate.shape[0]
    width = w_gate.shape[1]
    shard_at, inner_at = lax.axis_index("shard"), lax.axis_index("inner")

    ids = owners[:, 0] * own_items + item_rows
    position = jnp.arange(row_count, dtype=jnp.int32) % HIST_LEN
    limit_of = jnp.repeat(lengths, HIST_LEN, total_repeat_length=row_count)
    selector = (
        (ids[:, None] == jnp.arange(items, dtype=jnp.int32)[None, :])
        & (position < limit_of)[:, None]
    ).astype(jnp.bfloat16)

    slot_sums = lax.dot_general(
        selector, d_hidden, (((0,), (0,)), ((), ())), preferred_element_type=jnp.float32
    )
    item_cot = lax.psum(slot_sums.astype(jnp.bfloat16), "shard").astype(jnp.float32)

    embedded = jnp.dot(item_last, adapter, preferred_element_type=jnp.float32).astype(jnp.bfloat16)
    whole_rows = lax.all_gather(embedded, "inner", axis=1, tiled=True)
    block = lax.all_to_all(whole_rows, "shard", split_axis=1, concat_axis=0, tiled=True)
    block_f = block.astype(jnp.float32)
    gain_block = lax.dynamic_slice_in_dim(user_gain, shard_at * weight_rows, weight_rows, 0)
    squares = lax.psum(jnp.sum(block_f * block_f, axis=1), "shard")
    inv_rms = lax.rsqrt(squares / model_width + epsilon)
    scaled = (block_f * gain_block[None, :]).astype(jnp.bfloat16)
    partial_acts = jnp.concatenate(
        [
            jnp.dot(scaled, w_gate, preferred_element_type=jnp.float32).astype(jnp.bfloat16),
            jnp.dot(scaled, w_up, preferred_element_type=jnp.float32).astype(jnp.bfloat16),
        ],
        axis=1,
    )
    acts = lax.psum(partial_acts, "shard").astype(jnp.float32) * inv_rms[:, None]
    gate_act, up_act = acts[:, :width], acts[:, width:]
    sigmoid_gate = jax.nn.sigmoid(gate_act)
    active = gate_act * sigmoid_gate
    item_hidden = (active * up_act).astype(jnp.bfloat16)
    hidden = jnp.dot(selector, item_hidden, preferred_element_type=jnp.float32).astype(jnp.bfloat16)

    d_gate = item_cot * up_act * sigmoid_gate * (1.0 + gate_act * (1.0 - sigmoid_gate))
    d_up = item_cot * active
    dots = lax.psum(jnp.sum(d_gate * gate_act + d_up * up_act, axis=1), "inner")
    terms = contract_rows(d_gate.astype(jnp.bfloat16), w_gate) + contract_rows(
        d_up.astype(jnp.bfloat16), w_up
    )
    own_terms = lax.all_to_all(
        terms.astype(jnp.bfloat16), "shard", split_axis=0, concat_axis=1, tiled=True
    )
    d_normed = lax.psum_scatter(
        own_terms, "inner", scatter_dimension=1, tiled=True
    ).astype(jnp.float32)
    gain_own = lax.dynamic_slice_in_dim(user_gain, inner_at * own_width, own_width, 0)
    inv_own = lax.dynamic_slice_in_dim(inv_rms, shard_at * own_items, own_items, 0)[:, None]
    dots_own = lax.dynamic_slice_in_dim(dots, shard_at * own_items, own_items, 0)[:, None]
    item_grad = inv_own * gain_own[None, :] * d_normed - embedded.astype(jnp.float32) * (
        inv_own * inv_own * dots_own / model_width
    )
    return (hidden, item_grad)


def solution(mesh):
    return jax.shard_map(
        body,
        mesh=mesh,
        in_specs=(
            P(("groups", "shard"), None),
            P(None, "inner"),
            P(),
            P("shard", "inner"),
            P("shard", "inner"),
            P(("groups", "shard"), None),
            P(("groups", "shard")),
            P(("groups", "shard")),
            P(("groups", "shard"), "inner"),
        ),
        out_specs=(P(("groups", "shard"), "inner"), P(("groups", "shard"), "inner")),
        check_vma=False,
    )
```

time: 577 us -> 140 us (0.24)
  waiting for transfers between devices: 490 us -> 70.1 us
  matrix products: 35.4 us -> 15.4 us
  blocking collectives: 15.6 us -> 22.7 us
    all_gather x3 -> x0, waiting for transfers between devices: 446 us -> none  [the longest x1 218 us: body(): lax.all_gather(w_gate, 'shard', axis=0, tiled=True)]
    psum x1, waiting for transfers between devices: 29.2 us -> 45.4 us  [body(): lax.psum(partial_acts, 'shard').astype(jnp.float32) * inv_rms[:, None]]
    psum x0 -> x2, blocking collectives: none -> 15.5 us  [the longest x1 9.88 us: body(): squares = lax.psum(jnp.sum(block_f * block_f, axis=1), 'shard')]
    dot_general x2, matrix products: 17.1 us -> 4.45 us  [contract_rows(): lax.dot_general(left_side, right_side, (((1,), (1,)), ((), ())), preferre...]
    reduce_scatter x0 -> x1, waiting for transfers between devices: none -> 8.94 us  [body(): lax.psum_scatter(own_terms, 'inner', scatter_dimension=1, tiled=True)]
    all_gather x1, blocking collectives: 15.6 us -> 7.19 us  [body(): whole_rows = lax.all_gather(embedded, 'inner', axis=1, tiled=True)]
    dot_general x3 -> x4, matrix products: 15.3 us -> 7.72 us  [the longest x1 2.53 us: body(): jnp.dot(selector, item_hidden, preferred_element_type=jnp.float32)]
  transfers between devices with their start and end apart: 6 -> 4, of which waited for: 5 -> 4; matrix products, arithmetic and copies ran while one was open for 3% -> 5% of each run, Pallas kernels for 0% -> 0%
where the time goes in v1:
time: 140 us; the launch traced here: 139 us
  waiting for transfers between devices  70.1 us (50%)
  blocking collectives  22.7 us (16%)
  matrix products  15.4 us (11%)
  between operations  14.9 us (11%)
  starting transfers between devices  8.36 us (6%)
  other arithmetic  6.19 us (4%)
  local copies, waits for them, and re-layouts  1.57 us (1%)
    psum x1, waiting for transfers between devices, body(): lax.psum(partial_acts, 'shard').astype(jnp.float32) * inv_rms[:, None]  45.4 us
    psum x1, blocking collectives, body(): squares = lax.psum(jnp.sum(block_f * block_f, axis=1), 'shard')  9.88 us
    all_to_all x1, waiting for transfers between devices, body(): lax.all_to_all(terms.astype(jnp.bfloat16), 'shard', split_axis=0, concat_...  9.27 us
    reduce_scatter x1, waiting for transfers between devices, body(): lax.psum_scatter(own_terms, 'inner', scatter_dimension=1, tiled=True)  8.94 us
    all_gather x1, blocking collectives, body(): whole_rows = lax.all_gather(embedded, 'inner', axis=1, tiled=True)  7.19 us
    all_to_all x1, waiting for transfers between devices, body(): lax.all_to_all(whole_rows, 'shard', split_axis=1, concat_axis=0, tiled=True)  6.52 us
    psum x1, blocking collectives, body(): dots = lax.psum(jnp.sum(d_gate * gate_act + d_up * up_act, axis=1), 'inner')  5.66 us
    all_to_all x1, starting transfers between devices, body(): lax.all_to_all(whole_rows, 'shard', split_axis=1, concat_axis=0, tiled=True)  4.91 us
  transfers between devices with their start and end apart: 4, of which 4 were waited for; matrix products, arithmetic and copies ran while one was open for 5% of the time, Pallas kernels for 0%

profile of v1, /device:TPU:0, one launch (start us, length us, event | category | flops | bytes accessed | tf_op | source)
XLA Modules:
  0.0 139.3 jit_solution(14328430497754352483)
XLA Ops:
  7.2 3.2 %convolution_convert_fusion.4 = bf16[32,1024]{1,0:T(8,128)(2,1)S(1)} fusion(bf16[32,2048]{1,0:T(8,128)(2,1)} %param.13, bf16[2048,1024]{1,0:T(8,128)(2,1)} %param.14), kind=kOutput, calls=%fused_computation.7 | convolution fusion | flops 134250496 | bytes 4390912 | tf_op jit(solution)/shard_map/dot_general | solution.py:43
  10.4 7.2 %all_gather.3 = bf16[32,4096]{1,0:T(8,128)(2,1)S(1)} all-gather(bf16[32,1024]{1,0:T(8,128)(2,1)S(1)} %convolution_convert_fusion.4), channel_id=1, replica_groups=mesh['groups'=2,'shard'=4,'inner'=4] {'inner'}, dimensions={1}, use_global_device_ids=true | all-gather | bytes 327680 | tf_op jit(solution)/shard_map/all_gather | solution.py:44
  17.6 0.7 copy.19
  18.3 4.9 %all-to-all-start = ((bf16[32,4,1024]{2,0,1:T(8,128)(2,1)}), bf16[32,4,1024]{2,0,1:T(8,128)(2,1)S(1)}, u32[]{:S(2)}, u32[]{:S(2)}) async-start(bf16[32,4,1024]{2,0,1:T(8,128)(2,1)} %bitcast.29), calls=%async_computation | async-start | bytes 524288 | tf_op jit(solution)/shard_map/all_to_all | solution.py:45
  24.0 2.1 %convolution_convert_fusion = bf16[128,1536]{1,0:T(8,128)(2,1)} fusion(bf16[128,1536]{1,0:T(8,128)(2,1)} %param.21, s32[128]{0:T(128)S(1)} %bitcast_add_fusion, pred[128]{0:T(512)(128)(4,1)S(1)} %fusion.16), kind=kOutput, calls=%fused_computation | convolution fusion | flops 50561024 | bytes 787072 | tf_op jit(solution)/shard_map/dot_general | solution.py:38
  26.1 6.5 %all-to-all-done = bf16[32,4,1024]{2,0,1:T(8,128)(2,1)S(1)} async-done(((bf16[32,4,1024]{2,0,1:T(8,128)(2,1)}), bf16[32,4,1024]{2,0,1:T(8,128)(2,1)S(1)}, u32[]{:S(2)}, u32[]{:S(2)}) %all-to-all-start) | async-done | bytes 262176 | tf_op jit(solution)/shard_map/all_to_all | solution.py:45
  32.7 2.5 %convolution_convert_fusion.2 = bf16[128,1536]{1,0:T(8,128)(2,1)S(1)} fusion(bf16[128,1024]{1,0:T(8,128)(2,1)S(1)} %fusion.5, bf16[1024,1536]{1,0:T(8,128)(2,1)} %param.17), kind=kOutput, calls=%fused_computation.2 | convolution fusion | flops 402849792 | bytes 3801088 | tf_op jit(solution)/shard_map/dot_general | solution.py:54
  35.2 0.6 convolution_convert_fusion.3
  35.8 1.0 pad_maximum_fusion
  36.8 0.1 multiply_reduce_fusion
  36.9 0.1 reduce_sum.24
  37.0 9.9 %psum.29 = f32[128]{0:T(128)S(1)} all-reduce(f32[128]{0:T(128)S(1)} %reduce_sum.24), channel_id=1, replica_groups=mesh['groups'=2,'shard'=4,'inner'=4] {'shard'}, use_global_device_ids=true, to_apply=%region_2.3 | all-reduce | flops 128 | bytes 1024 | tf_op jit(solution)/shard_map/psum | solution.py:48
  46.9 45.4 %all-reduce.3.cloned.1.call-done = (bf16[128,3072]{1,0:T(8,128)(2,1)}, bf16[128,1536]{1,0:T(8,128)(2,1)}) async-done(((bf16[128,3072]{1,0:T(8,128)(2,1)}, bf16[128,1536]{1,0:T(8,128)(2,1)}), (bf16[128,3072]{1,0:T(8,128)(2,1)}, bf16[128,1536]{1,0:T(8,128)(2,1)})) %all-reduce.3.cloned.1.call-update) | async-done | bytes 1179664 | tf_op jit(solution)/shard_map/psum | solution.py:58
  92.3 1.3 convert_multiply_fusion
  93.6 2.6 %fusion.7 = f32[128,1024]{1,0:T(8,128)S(1)} fusion(bf16[1024,1536]{1,0:T(8,128)(2,1)S(1)} %copy-done, bf16[128,1536]{1,0:T(8,128)(2,1)} %get-tuple-element.27, f32[128,3072]{1,0:T(8,128)S(1)} %convert_multiply_fusion), kind=kOutput, calls=%fused_computation.21 | convolution fusion | flops 404815872 | bytes 5636096 | tf_op jit(solution)/shard_map/dot_general | solution.py:13
  96.3 1.9 %fusion = bf16[128,1024]{1,0:T(8,128)(2,1)} fusion(f32[128,1024]{1,0:T(8,128)S(1)} %fusion.7, bf16[1024,1536]{1,0:T(8,128)(2,1)S(1)} %copy-done.2, bf16[128,1536]{1,0:T(8,128)(2,1)S(1)} %copy-done.3, f32[128,3072]{1,0:T(8,128)S(1)} %convert_multiply_fusion), kind=kOutput, calls=%fused_computation.6 | convolution fusion | flops 404291584 | bytes 5111808 | tf_op jit(solution)/shard_map/dot_general | solution.py:13
  98.1 3.4 %all-to-all-start.1 = ((bf16[4,32,1024]{2,1,0:T(8,128)(2,1)}), bf16[4,32,1024]{2,1,0:T(8,128)(2,1)S(1)}, u32[]{:S(2)}, u32[]{:S(2)}) async-start(bf16[4,32,1024]{2,1,0:T(8,128)(2,1)} %bitcast.32), calls=%async_computation.1 | async-start | bytes 524288 | tf_op jit(solution)/shard_map/all_to_all | solution.py:71
  101.6 9.3 %all-to-all-done.1 = bf16[4,32,1024]{2,1,0:T(8,128)(2,1)S(1)} async-done(((bf16[4,32,1024]{2,1,0:T(8,128)(2,1)}), bf16[4,32,1024]{2,1,0:T(8,128)(2,1)S(1)}, u32[]{:S(2)}, u32[]{:S(2)}) %all-to-all-start.1) | async-done | bytes 262176 | tf_op jit(solution)/shard_map/all_to_all | solution.py:71
  110.9 0.7 copy.17
  111.6 2.0 %add_reduce_fusion = f32[128]{0:T(128)S(1)} fusion(f32[128,3072]{1,0:T(8,128)} %copy-done.1, bf16[128,1536]{1,0:T(8,128)(2,1)} %get-tuple-element.27), kind=kLoop, calls=%fused_computation.13 | loop fusion | flops 3145600 | bytes 1966592 | tf_op jit(solution)/shard_map/reduce_sum | solution.py:67
  113.6 5.7 %psum.31 = f32[128]{0:T(128)S(1)} all-reduce(f32[128]{0:T(128)S(1)} %add_reduce_fusion), channel_id=1, replica_groups=mesh['groups'=2,'shard'=4,'inner'=4] {'inner'}, use_global_device_ids=true, to_apply=%region_6.7 | all-reduce | flops 128 | bytes 1024 | tf_op jit(solution)/shard_map/psum | solution.py:67
  119.4 2.5 %convolution_convert_fusion.1 = bf16[128,1536]{1,0:T(8,128)(2,1)} fusion(f32[128,3072]{1,0:T(8,128)} %copy-done.1, s32[128]{0:T(128)S(1)} %bitcast_add_fusion, pred[128]{0:T(512)(128)(4,1)S(1)} %fusion.16), kind=kOutput, calls=%fused_computation.1 | convolution fusion | flops 51740672 | bytes 1966720 | tf_op jit(solution)/shard_map/dot_general | solution.py:63
  121.9 8.9 %reduce-scatter.2.cloned.1.call-done = bf16[32,1024]{1,0:T(8,128)(2,1)} async-done(((bf16[32,4096]{1,0:T(8,128)(2,1)}), bf16[32,1024]{1,0:T(8,128)(2,1)}) %reduce-scatter.2.cloned.1.call-update) | async-done | bytes 65552 | tf_op jit(solution)/shard_map/reduce_scatter | solution.py:74
  130.9 1.6 %multiply_subtract_fusion = f32[32,1024]{1,0:T(8,128)} fusion(bf16[32,1024]{1,0:T(8,128)(2,1)S(1)} %convolution_convert_fusion.4, bf16[32,1024]{1,0:T(8,128)(2,1)} %reduce-scatter.2.cloned.1.call-done, f32[32]{0:T(128)S(1)} %get-tuple-element.28, f32[1024]{0:T(1024)S(1)} %get-tuple-element.30, f32[32]{0:T(128)S(1)} %get-tuple-element.29), kind=kLoop, calls=%fused_computation.24 | loop fusion | flops 196608 | bytes 266496 | tf_op jit(solution)/shard_map/sub | solution.py:80
  (24 shorter events, 0.3 us)
Async XLA Ops:
  7.2 28.0 %copy-start = (bf16[1024,1536]{1,0:T(8,128)(2,1)S(1)}, bf16[1024,1536]{1,0:T(8,128)(2,1)}, u32[]{:S(2)}) copy-start(bf16[1024,1536]{1,0:T(8,128)(2,1)} %param.16) | copy-start | bytes 9437188
  7.2 16.7 %copy-start.6 = (s32[128,1]{0,1:T(1,128)S(1)}, s32[128,1]{0,1:T(1,128)}, u32[]{:S(2)}) copy-start(s32[128,1]{0,1:T(1,128)} %param.18) | copy-start | bytes 1540
  7.2 16.7 %copy-start.5 = (s32[128]{0:T(128)S(1)}, s32[128]{0:T(128)}, u32[]{:S(2)}) copy-start(s32[128]{0:T(128)} %param.19) | copy-start | bytes 1540
  7.2 16.8 %copy-start.4 = (f32[4096]{0:T(1024)S(1)}, f32[4096]{0:T(1024)}, u32[]{:S(2)}) copy-start(f32[4096]{0:T(1024)} %param.15) | copy-start | bytes 49156
  18.3 14.3 %all-to-all-start = ((bf16[32,4,1024]{2,0,1:T(8,128)(2,1)}), bf16[32,4,1024]{2,0,1:T(8,128)(2,1)S(1)}, u32[]{:S(2)}, u32[]{:S(2)}) async-start(bf16[32,4,1024]{2,0,1:T(8,128)(2,1)} %bitcast.29), calls=%async_computation | async-start | bytes 524288 | tf_op jit(solution)/shard_map/all_to_all | solution.py:45
  23.3 69.0 %all-reduce.3.cloned.1.call-start = ((), (), s32[]{:S(2)}) async-start(), calls=%async_computation.4 | async-start | bytes 2359296 | tf_op jit(solution)/shard_map/psum | solution.py:58
  93.6 2.6 %copy-start.1 = (f32[128,3072]{1,0:T(8,128)}, f32[128,3072]{1,0:T(8,128)S(1)}, u32[]{:S(2)}) copy-start(f32[128,3072]{1,0:T(8,128)S(1)} %convert_multiply_fusion) | copy-start | bytes 4718596
  93.6 2.6 %copy-start.2 = (bf16[1024,1536]{1,0:T(8,128)(2,1)S(1)}, bf16[1024,1536]{1,0:T(8,128)(2,1)}, u32[]{:S(2)}) copy-start(bf16[1024,1536]{1,0:T(8,128)(2,1)} %param.17) | copy-start | bytes 9437188
  93.6 2.6 %copy-start.3 = (bf16[128,1536]{1,0:T(8,128)(2,1)S(1)}, bf16[128,1536]{1,0:T(8,128)(2,1)}, u32[]{:S(2)}) copy-start(bf16[128,1536]{1,0:T(8,128)(2,1)} %get-tuple-element.27) | copy-start | bytes 1179652
  98.1 12.7 %all-to-all-start.1 = ((bf16[4,32,1024]{2,1,0:T(8,128)(2,1)}), bf16[4,32,1024]{2,1,0:T(8,128)(2,1)S(1)}, u32[]{:S(2)}, u32[]{:S(2)}) async-start(bf16[4,32,1024]{2,1,0:T(8,128)(2,1)} %bitcast.32), calls=%async_computation.1 | async-start | bytes 524288 | tf_op jit(solution)/shard_map/all_to_all | solution.py:71
  101.5 29.3 %reduce-scatter.2.cloned.1.call-start = ((), (), s32[]{:S(2)}) async-start(), calls=%async_computation.3 | async-start | bytes 327680 | tf_op jit(solution)/shard_map/reduce_scatter | solution.py:74
Sparse Core Ops, SparseCore 0:
  36.9 55.3 all-reduce.2
  111.7 19.0 reduce-scatter.1

commit v2 on v1

--- a/solution.py
+++ b/solution.py
@@ -1,6 +1,11 @@
+import functools
+import math
+
 import jax
 import jax.numpy as jnp
 from jax import lax
+from jax.experimental import pallas as pl
+from jax.experimental.pallas import tpu as pltpu
 from jax.sharding import PartitionSpec as P
 
 HIST_LEN = 128
@@ -83,9 +88,352 @@
     return (hidden, item_grad)
 
 
+def square_kernel(
+    n, ids_ref, item_ref, gain_ref, adapter_hbm, cot_hbm, gate_hbm, up_hbm,
+    hidden_ref, grad_ref,
+    adapter, cot, w_gate, w_up, own, block, scaled, cot_out, cot_in, act_out, act_in,
+    squares, dots, grads_all, hidden_all, terms_out, terms_in,
+    load_sem, own_send, own_recv, sq_send, sq_recv, cot_send, cot_recv, act_send, act_recv,
+    grads_send, grads_recv, hid_send, hid_recv, dots_send, dots_recv, terms_send, terms_recv,
+):
+    s, i = lax.axis_index("shard"), lax.axis_index("inner")
+    on_diagonal = s == i
+    rows, own_width = own.shape
+    items, width = cot_out.shape
+    depth = block.shape[1]
+    model_width = own_width * n
+
+    def shifted(base, by):
+        return lax.rem(base + by, n)
+
+    def part(index):
+        return pl.ds(pl.multiple_of(index * rows, rows), rows)
+
+    def device(shard, inner):
+        return {"shard": shard, "inner": inner}
+
+    def send(src, dst, send_sem, recv_sem, shard, inner):
+        return pltpu.make_async_remote_copy(
+            src_ref=src, dst_ref=dst, send_sem=send_sem, recv_sem=recv_sem,
+            device_id=device(shard, inner), device_id_type=pl.DeviceIdType.MESH,
+        )
+
+    loads = [
+        pltpu.make_async_copy(src, dst, load_sem.at[k])
+        for k, (src, dst) in enumerate(
+            [(adapter_hbm, adapter), (cot_hbm, cot), (gate_hbm, w_gate), (up_hbm, w_up)]
+        )
+    ]
+    for load in loads:
+        load.start()
+
+    barrier = pltpu.get_barrier_semaphore()
+
+    def greet(shard, inner):
+        pl.semaphore_signal(
+            barrier, inc=1, device_id=device(shard, inner), device_id_type=pl.DeviceIdType.MESH
+        )
+
+    for r in range(1, n):
+        greet(shifted(s, r), i)
+        greet(s, shifted(i, r))
+
+    @pl.when(jnp.logical_not(on_diagonal))
+    def _():
+        for r in range(1, n):
+            greet(i, shifted(i, r))
+            pl.when(shifted(s, r) != i)(functools.partial(greet, shifted(s, r), s))
+
+    loads[0].wait()
+    tile = math.gcd(own_width, 256)
+
+    def embed(c, carry):
+        at = pl.ds(pl.multiple_of(c * tile, tile), tile)
+        own[:, at] = jnp.dot(
+            item_ref[...], adapter[:, at], preferred_element_type=jnp.float32
+        ).astype(jnp.bfloat16)
+        return carry
+
+    lax.fori_loop(0, own_width // tile, embed, 0)
+    own_f = own[...].astype(jnp.float32)
+    squares[0] = jnp.broadcast_to(jnp.sum(own_f * own_f, axis=1, keepdims=True), (rows, 128))
+
+    @pl.when(on_diagonal)
+    def _():
+        pl.semaphore_wait(barrier, 2 * (n - 1))
+
+    @pl.when(jnp.logical_not(on_diagonal))
+    def _():
+        pl.semaphore_wait(barrier, 4 * (n - 1) - 1)
+
+    own_copies = [
+        send(own, block.at[part(s)], own_send.at[r], own_recv.at[s], i, shifted(i, r))
+        for r in range(n)
+    ]
+    for copy in own_copies[1:]:
+        copy.start()
+
+    @pl.when(jnp.logical_not(on_diagonal))
+    def _():
+        own_copies[0].start()
+
+    @pl.when(on_diagonal)
+    def _():
+        block[part(s), :] = own[...]
+
+    sq_copies = [
+        send(squares.at[0], squares.at[r], sq_send.at[r - 1], sq_recv.at[r - 1], s, shifted(i, r))
+        for r in range(1, n)
+    ]
+    for copy in sq_copies:
+        copy.start()
+
+    chosen = (
+        lax.broadcasted_iota(jnp.int32, (items, ids_ref.shape[1]), 0) == ids_ref[...]
+    ).astype(jnp.float32).astype(jnp.bfloat16)
+    loads[1].wait()
+    wide = math.gcd(width, 512)
+    for c in range(width // wide):
+        at = pl.ds(c * wide, wide)
+        cot_out[:, at] = jnp.dot(
+            chosen, cot[:, at], preferred_element_type=jnp.float32
+        ).astype(jnp.bfloat16)
+    cot_copies = [
+        send(
+            cot_out.at[part(shifted(s, r))], cot_in.at[r - 1],
+            cot_send.at[r - 1], cot_recv.at[r - 1], shifted(s, r), i,
+        )
+        for r in range(1, n)
+    ]
+    for copy in cot_copies:
+        copy.start()
+
+    for r in range(n):
+        source = shifted(s, r)
+        arrival = send(own, block.at[part(source)], own_send.at[r], own_recv.at[source], source, s)
+        if r == 0:
+            pl.when(jnp.logical_not(on_diagonal))(arrival.wait_recv)
+        else:
+            arrival.wait_recv()
+    scaled[...] = (block[...].astype(jnp.float32) * gain_ref[pl.ds(s, 1), :]).astype(jnp.bfloat16)
+    loads[2].wait()
+    loads[3].wait()
+    narrow = math.gcd(width, 256)
+
+    def activate(c, carry):
+        at = pl.ds(pl.multiple_of(c * narrow, narrow), narrow)
+        up_at = pl.ds(pl.multiple_of(c * narrow + width, narrow), narrow)
+        act_out[:, at] = jnp.dot(
+            scaled[...], w_gate[:, at], preferred_element_type=jnp.float32
+        ).astype(jnp.bfloat16)
+        act_out[:, up_at] = jnp.dot(
+            scaled[...], w_up[:, at], preferred_element_type=jnp.float32
+        ).astype(jnp.bfloat16)
+        return carry
+
+    lax.fori_loop(0, width // narrow, activate, 0)
+    act_copies = [
+        send(
+            act_out.at[part(shifted(s, r))], act_in.at[r - 1],
+            act_send.at[r - 1], act_recv.at[r - 1], shifted(s, r), i,
+        )
+        for r in range(1, n)
+    ]
+    for copy in act_copies:
+        copy.start()
+
+    for copy in sq_copies:
+        copy.wait_recv()
+    total = squares[0]
+    for r in range(1, n):
+        total = total + squares[r]
+    inv_rms = lax.rsqrt(total[:, :1] / model_width + epsilon)
+
+    for copy in cot_copies + act_copies:
+        copy.wait_recv()
+    dot_sum = jnp.zeros((rows, 1), jnp.float32)
+    for c in range(width // narrow):
+        at, up_at = pl.ds(c * narrow, narrow), pl.ds(c * narrow + width, narrow)
+
+        def whole(out_ref, in_ref, columns):
+            value = out_ref[part(s), columns].astype(jnp.float32)
+            for r in range(n - 1):
+                value = value + in_ref[r, :, columns].astype(jnp.float32)
+            return value
+
+        gate_act = whole(act_out, act_in, at) * inv_rms
+        up_act = whole(act_out, act_in, up_at) * inv_rms
+        item_cot = whole(cot_out, cot_in, at)
+        sigmoid_gate = jax.nn.sigmoid(gate_act)
+        active = gate_act * sigmoid_gate
+        hidden_all[part(s), at] = (active * up_act).astype(jnp.bfloat16)
+        d_gate = item_cot * up_act * sigmoid_gate * (1.0 + gate_act * (1.0 - sigmoid_gate))
+        d_up = item_cot * active
+        grads_all[part(s), at] = d_gate.astype(jnp.bfloat16)
+        grads_all[part(s), up_at] = d_up.astype(jnp.bfloat16)
+        dot_sum = dot_sum + jnp.sum(d_gate * gate_act + d_up * up_act, axis=1, keepdims=True)
+    grads_copies = [
+        send(
+            grads_all.at[part(s)], grads_all.at[part(s)],
+            grads_send.at[r - 1], grads_recv.at[r - 1], shifted(s, r), i,
+        )
+        for r in range(1, n)
+    ]
+    hid_copies = [
+        send(
+            hidden_all.at[part(s)], hidden_all.at[part(s)],
+            hid_send.at[r - 1], hid_recv.at[r - 1], shifted(s, r), i,
+        )
+        for r in range(1, n)
+    ]
+    for copy in grads_copies:
+        copy.start()
+    dots[0] = jnp.broadcast_to(dot_sum, (rows, 128))
+    dots_copies = [
+        send(dots.at[0], dots.at[r], dots_send.at[r - 1], dots_recv.at[r - 1], s, shifted(i, r))
+        for r in range(1, n)
+    ]
+    for copy in dots_copies + hid_copies:
+        copy.start()
+
+    for copy in grads_copies:
+        copy.wait_recv()
+    high = math.gcd(depth, 256)
+
+    def contract(c, carry):
+        at = pl.ds(pl.multiple_of(c * high, high), high)
+        terms_out[:, at] = (
+            contract_rows(grads_all[:, :width], w_gate[at, :])
+            + contract_rows(grads_all[:, width:], w_up[at, :])
+        ).astype(jnp.bfloat16)
+        return carry
+
+    lax.fori_loop(0, depth // high, contract, 0)
+    terms_copies = [
+        send(
+            terms_out.at[part(shifted(s, r))], terms_in.at[i],
+            terms_send.at[r], terms_recv.at[i], shifted(s, r), s,
+        )
+        for r in range(n)
+    ]
+    for copy in terms_copies[1:]:
+        copy.start()
+
+    @pl.when(jnp.logical_not(on_diagonal))
+    def _():
+        terms_copies[0].start()
+
+    @pl.when(on_diagonal)
+    def _():
+        terms_in[i] = terms_out[part(s), :]
+
+    for copy in hid_copies:
+        copy.wait_recv()
+    for c in range(width // wide):
+        at = pl.ds(c * wide, wide)
+        hidden_ref[:, at] = lax.dot_general(
+            chosen, hidden_all[:, at], (((0,), (0,)), ((), ())), preferred_element_type=jnp.float32
+        ).astype(jnp.bfloat16)
+
+    for copy in dots_copies:
+        copy.wait_recv()
+    total = dots[0]
+    for r in range(1, n):
+        total = total + dots[r]
+    shrink = inv_rms * inv_rms * total[:, :1] / model_width
+    for r in range(n):
+        source = shifted(i, r)
+        arrival = send(
+            terms_out.at[part(s)], terms_in.at[source], terms_send.at[r], terms_recv.at[source],
+            i, source,
+        )
+        if r == 0:
+            pl.when(jnp.logical_not(on_diagonal))(arrival.wait_recv)
+        else:
+            arrival.wait_recv()
+    d_normed = terms_in[0].astype(jnp.float32)
+    for r in range(1, n):
+        d_normed = d_normed + terms_in[r].astype(jnp.float32)
+    grad_ref[...] = inv_rms * gain_ref[pl.ds(i, 1), :] * d_normed - own[...].astype(
+        jnp.float32
+    ) * shrink
+
+    for copy in (
+        sq_copies + cot_copies + act_copies + grads_copies + hid_copies + dots_copies
+        + own_copies[1:] + terms_copies[1:]
+    ):
+        copy.wait_send()
+
+    @pl.when(jnp.logical_not(on_diagonal))
+    def _():
+        own_copies[0].wait_send()
+        terms_copies[0].wait_send()
+
+
+def square_body(item_last, adapter, user_gain, w_gate, w_up, owners, item_rows, lengths, d_hidden):
+    n = lax.axis_size("shard")
+    rows, item_width = item_last.shape
+    items = rows * n
+    row_count = owners.shape[0]
+    model_width = user_gain.shape[0]
+    own_width = model_width // n
+    depth, width = w_gate.shape
+    ids = owners.reshape(1, row_count) * rows + item_rows.reshape(1, row_count)
+    position = jnp.arange(row_count, dtype=jnp.int32) % HIST_LEN
+    limit_of = jnp.repeat(lengths, HIST_LEN, total_repeat_length=row_count)
+    ids = jnp.where((position < limit_of)[None, :], ids, -1)
+    bf16, f32 = jnp.bfloat16, jnp.float32
+    vmem, anywhere = pl.BlockSpec(memory_space=pltpu.VMEM), pl.BlockSpec(memory_space=pl.ANY)
+    sems = lambda count: pltpu.SemaphoreType.DMA((count,))
+    return pl.pallas_call(
+        functools.partial(square_kernel, n),
+        out_shape=(
+            jax.ShapeDtypeStruct((row_count, width), bf16),
+            jax.ShapeDtypeStruct((rows, own_width), f32),
+        ),
+        in_specs=[vmem] * 3 + [anywhere] * 4,
+        out_specs=(vmem, vmem),
+        scratch_shapes=[
+            pltpu.VMEM((item_width, own_width), bf16),
+            pltpu.VMEM((row_count, width), bf16),
+            pltpu.VMEM((depth, width), bf16),
+            pltpu.VMEM((depth, width), bf16),
+            pltpu.VMEM((rows, own_width), bf16),
+            pltpu.VMEM((items, depth), bf16),
+            pltpu.VMEM((items, depth), bf16),
+            pltpu.VMEM((items, width), bf16),
+            pltpu.VMEM((n - 1, rows, width), bf16),
+            pltpu.VMEM((items, 2 * width), bf16),
+            pltpu.VMEM((n - 1, rows, 2 * width), bf16),
+            pltpu.VMEM((n, rows, 128), f32),
+            pltpu.VMEM((n, rows, 128), f32),
+            pltpu.VMEM((items, 2 * width), bf16),
+            pltpu.VMEM((items, width), bf16),
+            pltpu.VMEM((items, depth), bf16),
+            pltpu.VMEM((n, rows, own_width), bf16),
+            sems(4),
+            sems(n), sems(n),
+            sems(n - 1), sems(n - 1),
+            sems(n - 1), sems(n - 1),
+            sems(n - 1), sems(n - 1),
+            sems(n - 1), sems(n - 1),
+            sems(n - 1), sems(n - 1),
+            sems(n - 1), sems(n - 1),
+            sems(n), sems(n),
+        ],
+        compiler_params=pltpu.CompilerParams(
+            collective_id=0, has_side_effects=True, vmem_limit_bytes=58 * 1024 * 1024
+        ),
+        cost_estimate=pl.CostEstimate(
+            flops=8 * items * depth * width, bytes_accessed=4 * depth * width, transcendentals=0
+        ),
+    )(ids, item_last, user_gain.reshape(n, own_width), adapter, d_hidden, w_gate, w_up)
+
+
 def solution(mesh):
+    square = mesh.shape["shard"] == mesh.shape["inner"]
     return jax.shard_map(
-        body,
+        square_body if square else body,
         mesh=mesh,
         in_specs=(
             P(("groups", "shard"), None),

time: 140 us -> 88.5 us (0.63)
  the two profiles are of different devices: /device:TPU:0 before, /device:TPU:15 now
where the time goes in v2:
time: 88.5 us; the launch traced here: 88.2 us
  Pallas kernels  81 us (92%)
  local copies, waits for them, and re-layouts  4.67 us (5%)
  between operations  1.29 us (1%)
  other arithmetic  1.19 us (1%)
    pallas_call x1, Pallas kernels, square_body(): pl.pallas_call(functools.partial(square_kernel, n), out_shape=(jax.ShapeD...  81 us
    unnamed x2, local copies, waits for them, and re-layouts  3.33 us

profile of v2, /device:TPU:15, one launch (start us, length us, event | category | flops | bytes accessed | tf_op | source)
XLA Modules:
  0.0 88.2 jit_solution(5711666541391021667)
XLA Ops:
  1.3 1.2 %fusion.ids_ref = s32[1,128]{1,0:T(1,128)} fusion(s32[128]{0:T(128)} %param.19, s32[128,1]{0,1:T(1,128)} %param.18, s32[]{:T(128)} %bitcast.9), kind=kLoop, calls=%fused_computation.3 | loop fusion | flops 1280 | bytes 1540 | tf_op jit(solution)/shard_map/jit(_where)/select_n | solution.py:384
  2.5 1.3 %reshape.80.gain_ref = f32[4,1024]{1,0:T(4,128)} reshape(f32[4096]{0:T(1024)} %param.15) | data formatting | bytes 32768 | tf_op jit(solution)/shard_map/reshape | solution.py:430
  3.8 81.0 %shard_map.107 = (bf16[128,1536]{1,0:T(8,128)(2,1)}, f32[32,1024]{1,0:T(8,128)}) custom-call(s32[1,128]{1,0:T(1,128)} %fusion.ids_ref, bf16[32,2048]{1,0:T(8,128)(2,1)} %item_ref.1, f32[4,1024]{1,0:T(4,128)} %reshape.80.gain_ref, bf16[2048,1024]{1,0:T(8,128)(2,1)} %adapter_hbm.1, bf16[128,1536]{1,0:T(8,128)(2,1)} %cot_hbm.1, bf16[1024,1536]{1,0:T(8,128)(2,1)} %gate_hbm.1, ...), custom_call_target="tpu_custom_call" | custom-call | flops 1610612736 | bytes 6291456 | tf_op jit(solution)/shard_map/pallas_call | solution.py:388
  84.9 1.8 %copy.14 = bf16[128,1536]{1,0:T(8,128)(2,1)} copy(bf16[128,1536]{1,0:T(8,128)(2,1)} %get-tuple-element.28) | data formatting | bytes 786432
  86.6 1.6 %copy.15 = f32[32,1024]{1,0:T(8,128)} copy(f32[32,1024]{1,0:T(8,128)} %get-tuple-element.29) | data formatting | bytes 262144

commit v3 on v2

v3 whole, which is shorter than its diff:
```python
import functools
import math

import jax
import jax.numpy as jnp
from jax import lax
from jax.experimental import pallas as pl
from jax.experimental.pallas import tpu as pltpu
from jax.sharding import PartitionSpec as P

HIST_LEN = 128


epsilon = 1e-05


def contract_rows(left_side, right_side):
    return lax.dot_general(
        left_side, right_side, (((1,), (1,)), ((), ())), preferred_element_type=jnp.float32
    )


def body(item_last, adapter, user_gain, w_gate, w_up, owners, item_rows, lengths, d_hidden):
    shards = lax.axis_size("shard")
    inner_count = lax.axis_size("inner")
    own_items = item_last.shape[0]
    items = own_items * shards
    row_count = owners.shape[0]
    model_width = user_gain.shape[0]
    own_width = model_width // inner_count
    weight_rows = w_gate.shape[0]
    width = w_gate.shape[1]
    shard_at, inner_at = lax.axis_index("shard"), lax.axis_index("inner")

    ids = owners[:, 0] * own_items + item_rows
    position = jnp.arange(row_count, dtype=jnp.int32) % HIST_LEN
    limit_of = jnp.repeat(lengths, HIST_LEN, total_repeat_length=row_count)
    selector = (
        (ids[:, None] == jnp.arange(items, dtype=jnp.int32)[None, :])
        & (position < limit_of)[:, None]
    ).astype(jnp.bfloat16)

    slot_sums = lax.dot_general(
        selector, d_hidden, (((0,), (0,)), ((), ())), preferred_element_type=jnp.float32
    )
    item_cot = lax.psum(slot_sums.astype(jnp.bfloat16), "shard").astype(jnp.float32)

    embedded = jnp.dot(item_last, adapter, preferred_element_type=jnp.float32).astype(jnp.bfloat16)
    whole_rows = lax.all_gather(embedded, "inner", axis=1, tiled=True)
    block = lax.all_to_all(whole_rows, "shard", split_axis=1, concat_axis=0, tiled=True)
    block_f = block.astype(jnp.float32)
    gain_block = lax.dynamic_slice_in_dim(user_gain, shard_at * weight_rows, weight_rows, 0)
    squares = lax.psum(jnp.sum(block_f * block_f, axis=1), "shard")
    inv_rms = lax.rsqrt(squares / model_width + epsilon)
    scaled = (block_f * gain_block[None, :]).astype(jnp.bfloat16)
    partial_acts = jnp.concatenate(
        [
            jnp.dot(scaled, w_gate, preferred_element_type=jnp.float32).astype(jnp.bfloat16),
            jnp.dot(scaled, w_up, preferred_element_type=jnp.float32).astype(jnp.bfloat16),
        ],
        axis=1,
    )
    acts = lax.psum(partial_acts, "shard").astype(jnp.float32) * inv_rms[:, None]
    gate_act, up_act = acts[:, :width], acts[:, width:]
    sigmoid_gate = jax.nn.sigmoid(gate_act)
    active = gate_act * sigmoid_gate
    item_hidden = (active * up_act).astype(jnp.bfloat16)
    hidden = jnp.dot(selector, item_hidden, preferred_element_type=jnp.float32).astype(jnp.bfloat16)

    d_gate = item_cot * up_act * sigmoid_gate * (1.0 + gate_act * (1.0 - sigmoid_gate))
    d_up = item_cot * active
    dots = lax.psum(jnp.sum(d_gate * gate_act + d_up * up_act, axis=1), "inner")
    terms = contract_rows(d_gate.astype(jnp.bfloat16), w_gate) + contract_rows(
        d_up.astype(jnp.bfloat16), w_up
    )
    own_terms = lax.all_to_all(
        terms.astype(jnp.bfloat16), "shard", split_axis=0, concat_axis=1, tiled=True
    )
    d_normed = lax.psum_scatter(
        own_terms, "inner", scatter_dimension=1, tiled=True
    ).astype(jnp.float32)
    gain_own = lax.dynamic_slice_in_dim(user_gain, inner_at * own_width, own_width, 0)
    inv_own = lax.dynamic_slice_in_dim(inv_rms, shard_at * own_items, own_items, 0)[:, None]
    dots_own = lax.dynamic_slice_in_dim(dots, shard_at * own_items, own_items, 0)[:, None]
    item_grad = inv_own * gain_own[None, :] * d_normed - embedded.astype(jnp.float32) * (
        inv_own * inv_own * dots_own / model_width
    )
    return (hidden, item_grad)


def line_kernel(
    n, owner_ref, row_ref, length_ref, item_ref, gain_ref, adapter_hbm, cot_hbm, gate_hbm, up_hbm,
    hidden_ref, grad_ref,
    adapter, cot, w_gate, w_up, own, block, scaled, squares, inv_all, dot_fold, dots,
    partial, outer_in, pair, other_in, total, terms, terms_out, terms_in,
    load_sem, own_send, own_recv, sq_send, sq_recv, inv_send, inv_recv, first_send, first_recv,
    second_send, second_recv, third_send, third_recv, dots_send, dots_recv, terms_send, terms_recv,
):
    s, i = lax.axis_index("shard"), lax.axis_index("inner")
    on_diagonal = s == i
    off_diagonal = jnp.logical_not(on_diagonal)
    at_end = jnp.logical_or(s == 0, s == n - 1)
    in_middle = jnp.logical_not(at_end)
    middle = 1 + s // (n - 1)
    outer, other = (s - 1) * (n - 1), n - 1 - s
    rows, own_width = own.shape
    items = block.shape[0]
    depth, width = w_gate.shape
    model_width = own_width * n
    piece = 512
    half = piece // 2
    cot_pieces, act_pieces = width // piece, width // half
    pieces = cot_pieces + act_pieces

    def shifted(base, by):
        return lax.rem(base + by, n)

    def part(index):
        return pl.ds(pl.multiple_of(index * rows, rows), rows)

    def device(shard, inner):
        return {"shard": shard, "inner": inner}

    def send(src, dst, send_sem, recv_sem, shard, inner):
        return pltpu.make_async_remote_copy(
            src_ref=src, dst_ref=dst, send_sem=send_sem, recv_sem=recv_sem,
            device_id=device(shard, inner), device_id_type=pl.DeviceIdType.MESH,
        )

    loads = [
        pltpu.make_async_copy(src, dst, load_sem.at[k])
        for k, (src, dst) in enumerate(
            [(adapter_hbm, adapter), (cot_hbm, cot), (gate_hbm, w_gate), (up_hbm, w_up)]
        )
    ]
    for load in loads:
        load.start()

    barrier = pltpu.get_barrier_semaphore()

    def greet(shard, inner):
        pl.semaphore_signal(
            barrier, inc=1, device_id=device(shard, inner), device_id_type=pl.DeviceIdType.MESH
        )

    for r in range(1, n):
        greet(shifted(s, r), i)
        greet(s, shifted(i, r))

    @pl.when(off_diagonal)
    def _():
        for r in range(1, n):
            greet(i, shifted(i, r))
            pl.when(shifted(s, r) != i)(functools.partial(greet, shifted(s, r), s))

    slots = owner_ref.shape[1]
    position = lax.broadcasted_iota(jnp.int32, (1, slots), 1)
    limit = jnp.zeros((1, slots), jnp.int32)
    for k in range(length_ref.shape[1]):
        limit = jnp.where(
            position >= k * HIST_LEN, length_ref[:, k : k + 1] + k * HIST_LEN, limit
        )
    ids = jnp.where(position < limit, owner_ref[...] * rows + row_ref[...], -1)
    chosen = (
        lax.broadcasted_iota(jnp.int32, (items, slots), 0) == ids
    ).astype(jnp.float32).astype(jnp.bfloat16)

    loads[0].wait()
    tile = math.gcd(own_width, 256)

    def embed(c, carry):
        at = pl.ds(pl.multiple_of(c * tile, tile), tile)
        own[:, at] = jnp.dot(
            item_ref[...], adapter[:, at], preferred_element_type=jnp.float32
        ).astype(jnp.bfloat16)
        return carry

    lax.fori_loop(0, own_width // tile, embed, 0)
    own_f = own[...].astype(jnp.float32)
    squares[0] = jnp.broadcast_to(jnp.sum(own_f * own_f, axis=1, keepdims=True), (rows, 128))

    @pl.when(on_diagonal)
    def _():
        pl.semaphore_wait(barrier, 2 * (n - 1))

    @pl.when(off_diagonal)
    def _():
        pl.semaphore_wait(barrier, 4 * (n - 1) - 1)

    own_copies = [
        send(own, block.at[part(s)], own_send.at[r], own_recv.at[s], i, shifted(i, r))
        for r in range(n)
    ]
    for copy in own_copies[1:]:
        copy.start()

    @pl.when(off_diagonal)
    def _():
        own_copies[0].start()

    @pl.when(on_diagonal)
    def _():
        block[part(s), :] = own[...]

    sq_copies = [
        send(squares.at[0], squares.at[r], sq_send.at[r - 1], sq_recv.at[r - 1], s, shifted(i, r))
        for r in range(1, n)
    ]
    for copy in sq_copies:
        copy.start()

    def columns(k):
        return pl.ds(k * piece, piece)

    def first(k, shard):
        at = columns(k)
        return send(
            partial.at[:, at], outer_in.at[:, at], first_send.at[k], first_recv.at[k], shard, i
        )

    def second(k):
        at = columns(k)
        return send(
            pair.at[:, at], other_in.at[:, at], second_send.at[k], second_recv.at[k], other, i
        )

    def third(k, shard):
        at = columns(k)
        return send(
            total.at[:, at], total.at[:, at], third_send.at[k], third_recv.at[k], shard, i
        )

    def added(left, right, at):
        return (left[:, at].astype(jnp.float32) + right[:, at].astype(jnp.float32)).astype(
            jnp.bfloat16
        )

    def pair_step(k):
        first(k, outer).wait_recv()
        pair[:, columns(k)] = added(partial, outer_in, columns(k))
        second(k).start()

    def total_step(k):
        second(k).wait_recv()
        total[:, columns(k)] = added(pair, other_in, columns(k))
        third(k, outer).start()

    loads[1].wait()
    for k in range(cot_pieces):
        partial[:, columns(k)] = jnp.dot(
            chosen, cot[:, columns(k)], preferred_element_type=jnp.float32
        ).astype(jnp.bfloat16)
        pl.when(at_end)(lambda k=k: first(k, middle).start())

    for copy in sq_copies:
        copy.wait_recv()
    square_sum = squares[0]
    for r in range(1, n):
        square_sum = square_sum + squares[r]
    inv_all[part(s), :] = lax.rsqrt(square_sum / model_width + epsilon)
    inv_copies = [
        send(
            inv_all.at[part(s)], inv_all.at[part(s)], inv_send.at[r - 1], inv_recv.at[r - 1],
            shifted(s, r), i,
        )
        for r in range(1, n)
    ]
    for copy in inv_copies:
        copy.start()

    @pl.when(in_middle)
    def _():
        for k in range(cot_pieces):
            pair_step(k)
            if k > 0:
                total_step(k - 1)

    for r in range(n):
        source = shifted(s, r)
        arrival = send(own, block.at[part(source)], own_send.at[r], own_recv.at[source], source, s)
        if r == 0:
            pl.when(off_diagonal)(arrival.wait_recv)
        else:
            arrival.wait_recv()
    depth_at = pl.ds(pl.multiple_of(s * depth, depth), depth)
    scaled[...] = (block[...].astype(jnp.float32) * gain_ref[:, depth_at]).astype(jnp.bfloat16)
    loads[2].wait()
    loads[3].wait()
    for copy in inv_copies:
        copy.wait_recv()

    def use(c):
        at = pl.ds(c * half, half)
        begin = (cot_pieces + c) * piece
        inv = inv_all[:, :1]
        gate_act = total[:, pl.ds(begin, half)].astype(jnp.float32) * inv
        up_act = total[:, pl.ds(begin + half, half)].astype(jnp.float32) * inv
        item_cot = total[:, at].astype(jnp.float32)
        sigmoid_gate = jax.nn.sigmoid(gate_act)
        active = gate_act * sigmoid_gate
        item_hidden = (active * up_act).astype(jnp.bfloat16)
        d_gate = item_cot * up_act * sigmoid_gate * (1.0 + gate_act * (1.0 - sigmoid_gate))
        d_up = item_cot * active
        product = d_gate * gate_act + d_up * up_act
        fold = product[:, :128]
        for k in range(1, half // 128):
            fold = fold + product[:, k * 128 : (k + 1) * 128]
        dot_fold[...] = fold if c == 0 else dot_fold[...] + fold
        term = contract_rows(d_gate.astype(jnp.bfloat16), w_gate[:, at]) + contract_rows(
            d_up.astype(jnp.bfloat16), w_up[:, at]
        )
        terms[...] = term if c == 0 else terms[...] + term
        hidden_ref[:, at] = lax.dot_general(
            chosen, item_hidden, (((0,), (0,)), ((), ())), preferred_element_type=jnp.float32
        ).astype(jnp.bfloat16)

    for c in range(act_pieces):
        k = cot_pieces + c
        at = pl.ds(c * half, half)
        for offset, weights in ((0, w_gate), (half, w_up)):
            partial[:, pl.ds(k * piece + offset, half)] = jnp.dot(
                scaled[...], weights[:, at], preferred_element_type=jnp.float32
            ).astype(jnp.bfloat16)
        pl.when(at_end)(lambda k=k: first(k, middle).start())

        @pl.when(in_middle)
        def _():
            pair_step(k)
            total_step(k - 1)
            if c > 0:
                use(c - 1)

    @pl.when(in_middle)
    def _():
        total_step(pieces - 1)
        use(act_pieces - 1)

    @pl.when(at_end)
    def _():
        for k in range(cot_pieces):
            third(k, middle).wait_recv()
        for c in range(act_pieces):
            third(cot_pieces + c, middle).wait_recv()
            use(c)

    terms_out[...] = terms[...].astype(jnp.bfloat16)
    terms_copies = [
        send(
            terms_out.at[part(shifted(s, r))], terms_in.at[i],
            terms_send.at[r], terms_recv.at[i], shifted(s, r), s,
        )
        for r in range(n)
    ]
    for copy in terms_copies[1:]:
        copy.start()

    @pl.when(off_diagonal)
    def _():
        terms_copies[0].start()

    @pl.when(on_diagonal)
    def _():
        terms_in[i] = terms_out[part(s), :]

    dots[0] = jnp.broadcast_to(
        jnp.sum(dot_fold[part(s), :], axis=1, keepdims=True), (rows, 128)
    )
    dots_copies = [
        send(dots.at[0], dots.at[r], dots_send.at[r - 1], dots_recv.at[r - 1], s, shifted(i, r))
        for r in range(1, n)
    ]
    for copy in dots_copies:
        copy.start()
    for copy in dots_copies:
        copy.wait_recv()
    dot_sum = dots[0]
    for r in range(1, n):
        dot_sum = dot_sum + dots[r]
    inv_own = inv_all[part(s), :][:, :1]
    shrink = inv_own * inv_own * dot_sum[:, :1] / model_width
    for r in range(n):
        source = shifted(i, r)
        arrival = send(
            terms_out.at[part(s)], terms_in.at[source], terms_send.at[r], terms_recv.at[source],
            i, source,
        )
        if r == 0:
            pl.when(off_diagonal)(arrival.wait_recv)
        else:
            arrival.wait_recv()
    d_normed = terms_in[0].astype(jnp.float32)
    for r in range(1, n):
        d_normed = d_normed + terms_in[r].astype(jnp.float32)
    own_at = pl.ds(pl.multiple_of(i * own_width, own_width), own_width)
    grad_ref[...] = inv_own * gain_ref[:, own_at] * d_normed - own[...].astype(
        jnp.float32
    ) * shrink

    for copy in sq_copies + inv_copies + dots_copies + own_copies[1:] + terms_copies[1:]:
        copy.wait_send()

    @pl.when(off_diagonal)
    def _():
        own_copies[0].wait_send()
        terms_copies[0].wait_send()

    @pl.when(at_end)
    def _():
        for k in range(pieces):
            first(k, middle).wait_send()

    @pl.when(in_middle)
    def _():
        for k in range(pieces):
            second(k).wait_send()
            third(k, outer).wait_send()


def line_body(item_last, adapter, user_gain, w_gate, w_up, owners, item_rows, lengths, d_hidden):
    n = lax.axis_size("shard")
    rows, item_width = item_last.shape
    items = rows * n
    row_count = owners.shape[0]
    own_width = user_gain.shape[0] // n
    depth, width = w_gate.shape
    bf16, f32 = jnp.bfloat16, jnp.float32
    vmem, anywhere = pl.BlockSpec(memory_space=pltpu.VMEM), pl.BlockSpec(memory_space=pl.ANY)
    sems = lambda count: pltpu.SemaphoreType.DMA((count,))
    pieces = width // 512 + width // 256
    sums = pltpu.VMEM((items, 3 * width), bf16)
    return pl.pallas_call(
        functools.partial(line_kernel, n),
        out_shape=(
            jax.ShapeDtypeStruct((row_count, width), bf16),
            jax.ShapeDtypeStruct((rows, own_width), f32),
        ),
        in_specs=[vmem] * 5 + [anywhere] * 4,
        out_specs=(vmem, vmem),
        scratch_shapes=[
            pltpu.VMEM((item_width, own_width), bf16),
            pltpu.VMEM((row_count, width), bf16),
            pltpu.VMEM((depth, width), bf16),
            pltpu.VMEM((depth, width), bf16),
            pltpu.VMEM((rows, own_width), bf16),
            pltpu.VMEM((items, depth), bf16),
            pltpu.VMEM((items, depth), bf16),
            pltpu.VMEM((n, rows, 128), f32),
            pltpu.VMEM((items, 128), f32),
            pltpu.VMEM((items, 128), f32),
            pltpu.VMEM((n, rows, 128), f32),
            sums, sums, sums, sums, sums,
            pltpu.VMEM((items, depth), f32),
            pltpu.VMEM((items, depth), bf16),
            pltpu.VMEM((n, rows, own_width), bf16),
            sems(4),
            sems(n), sems(n),
            sems(n - 1), sems(n - 1),
            sems(n - 1), sems(n - 1),
            sems(pieces), sems(pieces),
            sems(pieces), sems(pieces),
            sems(pieces), sems(pieces),
            sems(n - 1), sems(n - 1),
            sems(n), sems(n),
        ],
        compiler_params=pltpu.CompilerParams(
            collective_id=0, has_side_effects=True, vmem_limit_bytes=58 * 1024 * 1024
        ),
        cost_estimate=pl.CostEstimate(
            flops=8 * items * depth * width, bytes_accessed=4 * depth * width, transcendentals=0
        ),
    )(
        owners.reshape(1, -1), item_rows.reshape(1, -1), lengths.reshape(1, -1),
        item_last, user_gain.reshape(1, -1), adapter, d_hidden, w_gate, w_up,
    )


def solution(mesh):
    on_line = mesh.shape["shard"] == mesh.shape["inner"] == 4
    return jax.shard_map(
        line_body if on_line else body,
        mesh=mesh,
        in_specs=(
            P(("groups", "shard"), None),
            P(None, "inner"),
            P(),
            P("shard", "inner"),
            P("shard", "inner"),
            P(("groups", "shard"), None),
            P(("groups", "shard")),
            P(("groups", "shard")),
            P(("groups", "shard"), "inner"),
        ),
        out_specs=(P(("groups", "shard"), "inner"), P(("groups", "shard"), "inner")),
        check_vma=False,
    )
```

time: 88.5 us -> 66.3 us (0.75)
  the two profiles are of different devices: /device:TPU:15 before, /device:TPU:0 now
where the time goes in v3:
time: 66.3 us; the launch traced here: 66.1 us
  Pallas kernels  61.5 us (93%)
  local copies, waits for them, and re-layouts  3.33 us (5%)
  between operations  1.29 us (2%)
    pallas_call x1, Pallas kernels, line_body(): pl.pallas_call(functools.partial(line_kernel, n), out_shape=(jax.ShapeDty...  61.5 us
    unnamed x2, local copies, waits for them, and re-layouts  3.33 us

profile of v3, /device:TPU:0, one launch (start us, length us, event | category | flops | bytes accessed | tf_op | source)
XLA Modules:
  0.0 66.1 jit_solution(16650108189995026488)
XLA Ops:
  1.3 61.5 %shard_map.104 = (bf16[128,1536]{1,0:T(8,128)(2,1)}, f32[32,1024]{1,0:T(8,128)}) custom-call(s32[1,128]{1,0:T(1,128)} %bitcast.6, s32[1,128]{1,0:T(1,128)} %bitcast.7, s32[1,1]{1,0:T(1,128)} %bitcast.4.length_ref, bf16[32,2048]{1,0:T(8,128)(2,1)} %item_ref.1, f32[1,4096]{1,0:T(1,128)} %bitcast.5, bf16[2048,1024]{1,0:T(8,128)(2,1)} %adapter_hbm.1, ...), custom_call_target="tpu_custom_call" | custom-call | flops 1610612736 | bytes 6291456 | tf_op jit(solution)/shard_map/pallas_call | solution.py:431
  62.8 1.8 %copy.14 = bf16[128,1536]{1,0:T(8,128)(2,1)} copy(bf16[128,1536]{1,0:T(8,128)(2,1)} %get-tuple-element.4) | data formatting | bytes 786432
  64.6 1.6 %copy.15 = f32[32,1024]{1,0:T(8,128)} copy(f32[32,1024]{1,0:T(8,128)} %get-tuple-element.5) | data formatting | bytes 262144

commit v4 on v3

--- a/solution.py
+++ b/solution.py
@@ -93,12 +93,14 @@
     hidden_ref, grad_ref,
     adapter, cot, w_gate, w_up, own, block, scaled, squares, inv_all, dot_fold, dots,
     partial, outer_in, pair, other_in, total, terms, terms_out, terms_in,
-    load_sem, own_send, own_recv, sq_send, sq_recv, inv_send, inv_recv, first_send, first_recv,
+    load_sem, own_send, own_recv, relay_send, sq_send, sq_recv, inv_send, inv_recv, first_send, first_recv,
     second_send, second_recv, third_send, third_recv, dots_send, dots_recv, terms_send, terms_recv,
 ):
     s, i = lax.axis_index("shard"), lax.axis_index("inner")
     on_diagonal = s == i
     off_diagonal = jnp.logical_not(on_diagonal)
+    near = lax.rem(s + i, 2) == 0
+    sibling = i + 1 - 2 * lax.rem(i, 2)
     at_end = jnp.logical_or(s == 0, s == n - 1)
     in_middle = jnp.logical_not(at_end)
     middle = 1 + s // (n - 1)
@@ -130,7 +132,7 @@
     loads = [
         pltpu.make_async_copy(src, dst, load_sem.at[k])
         for k, (src, dst) in enumerate(
-            [(adapter_hbm, adapter), (cot_hbm, cot), (gate_hbm, w_gate), (up_hbm, w_up)]
+            [(cot_hbm, cot), (adapter_hbm, adapter), (gate_hbm, w_gate), (up_hbm, w_up)]
         )
     ]
     for load in loads:
@@ -165,7 +167,62 @@
         lax.broadcasted_iota(jnp.int32, (items, slots), 0) == ids
     ).astype(jnp.float32).astype(jnp.bfloat16)
 
+    def columns(k):
+        return pl.ds(k * piece, piece)
+
+    def first(k, shard):
+        at = columns(k)
+        return send(
+            partial.at[:, at], outer_in.at[:, at], first_send.at[k], first_recv.at[k], shard, i
+        )
+
+    def second(k):
+        at = columns(k)
+        return send(
+            pair.at[:, at], other_in.at[:, at], second_send.at[k], second_recv.at[k], other, i
+        )
+
+    def third(k, shard):
+        at = columns(k)
+        return send(
+            total.at[:, at], total.at[:, at], third_send.at[k], third_recv.at[k], shard, i
+        )
+
+    def added(left, right, at):
+        return (left[:, at].astype(jnp.float32) + right[:, at].astype(jnp.float32)).astype(
+            jnp.bfloat16
+        )
+
+    def pair_step(k):
+        first(k, outer).wait_recv()
+        pair[:, columns(k)] = added(partial, outer_in, columns(k))
+        second(k).start()
+
+    def total_step(k):
+        second(k).wait_recv()
+        total[:, columns(k)] = added(pair, other_in, columns(k))
+        third(k, outer).start()
+
     loads[0].wait()
+    for k in range(cot_pieces):
+        partial[:, columns(k)] = jnp.dot(
+            chosen, cot[:, columns(k)], preferred_element_type=jnp.float32
+        ).astype(jnp.bfloat16)
+
+    @pl.when(on_diagonal)
+    def _():
+        pl.semaphore_wait(barrier, 2 * (n - 1))
+
+    @pl.when(off_diagonal)
+    def _():
+        pl.semaphore_wait(barrier, 4 * (n - 1) - 1)
+
+    @pl.when(at_end)
+    def _():
+        for k in range(cot_pieces):
+            first(k, middle).start()
+
+    loads[1].wait()
     tile = math.gcd(own_width, 256)
 
     def embed(c, carry):
@@ -179,20 +236,11 @@
     own_f = own[...].astype(jnp.float32)
     squares[0] = jnp.broadcast_to(jnp.sum(own_f * own_f, axis=1, keepdims=True), (rows, 128))
 
-    @pl.when(on_diagonal)
-    def _():
-        pl.semaphore_wait(barrier, 2 * (n - 1))
-
-    @pl.when(off_diagonal)
-    def _():
-        pl.semaphore_wait(barrier, 4 * (n - 1) - 1)
-
     own_copies = [
-        send(own, block.at[part(s)], own_send.at[r], own_recv.at[s], i, shifted(i, r))
-        for r in range(n)
-    ]
-    for copy in own_copies[1:]:
-        copy.start()
+        send(own, block.at[part(s)], own_send.at[r // 2], own_recv.at[s], i, shifted(i, r))
+        for r in (0, 2)
+    ]
+    own_copies[1].start()
 
     @pl.when(off_diagonal)
     def _():
@@ -208,49 +256,6 @@
     ]
     for copy in sq_copies:
         copy.start()
-
-    def columns(k):
-        return pl.ds(k * piece, piece)
-
-    def first(k, shard):
-        at = columns(k)
-        return send(
-            partial.at[:, at], outer_in.at[:, at], first_send.at[k], first_recv.at[k], shard, i
-        )
-
-    def second(k):
-        at = columns(k)
-        return send(
-            pair.at[:, at], other_in.at[:, at], second_send.at[k], second_recv.at[k], other, i
-        )
-
-    def third(k, shard):
-        at = columns(k)
-        return send(
-            total.at[:, at], total.at[:, at], third_send.at[k], third_recv.at[k], shard, i
-        )
-
-    def added(left, right, at):
-        return (left[:, at].astype(jnp.float32) + right[:, at].astype(jnp.float32)).astype(
-            jnp.bfloat16
-        )
-
-    def pair_step(k):
-        first(k, outer).wait_recv()
-        pair[:, columns(k)] = added(partial, outer_in, columns(k))
-        second(k).start()
-
-    def total_step(k):
-        second(k).wait_recv()
-        total[:, columns(k)] = added(pair, other_in, columns(k))
-        third(k, outer).start()
-
-    loads[1].wait()
-    for k in range(cot_pieces):
-        partial[:, columns(k)] = jnp.dot(
-            chosen, cot[:, columns(k)], preferred_element_type=jnp.float32
-        ).astype(jnp.bfloat16)
-        pl.when(at_end)(lambda k=k: first(k, middle).start())
 
     for copy in sq_copies:
         copy.wait_recv()
@@ -270,18 +275,36 @@
 
     @pl.when(in_middle)
     def _():
-        for k in range(cot_pieces):
+        pair_step(0)
+
+    relays = [
+        send(
+            block.at[part(shifted(s, r))], block.at[part(shifted(s, r))],
+            relay_send.at[r], own_recv.at[shifted(s, r)], s, sibling,
+        )
+        for r in range(n)
+    ]
+
+    @pl.when(near)
+    def _():
+        for r in range(n):
+            if r == 0:
+                pl.when(off_diagonal)(relays[r].wait_recv)
+            else:
+                relays[r].wait_recv()
+            relays[r].start()
+
+    @pl.when(jnp.logical_not(near))
+    def _():
+        for r in range(n):
+            relays[r].wait_recv()
+
+    @pl.when(in_middle)
+    def _():
+        for k in range(1, cot_pieces):
             pair_step(k)
-            if k > 0:
-                total_step(k - 1)
-
-    for r in range(n):
-        source = shifted(s, r)
-        arrival = send(own, block.at[part(source)], own_send.at[r], own_recv.at[source], source, s)
-        if r == 0:
-            pl.when(off_diagonal)(arrival.wait_recv)
-        else:
-            arrival.wait_recv()
+            total_step(k - 1)
+
     depth_at = pl.ds(pl.multiple_of(s * depth, depth), depth)
     scaled[...] = (block[...].astype(jnp.float32) * gain_ref[:, depth_at]).astype(jnp.bfloat16)
     loads[2].wait()
@@ -343,6 +366,15 @@
             third(cot_pieces + c, middle).wait_recv()
             use(c)
 
+    dots[0] = jnp.broadcast_to(
+        jnp.sum(dot_fold[part(s), :], axis=1, keepdims=True), (rows, 128)
+    )
+    dots_copies = [
+        send(dots.at[0], dots.at[r], dots_send.at[r - 1], dots_recv.at[r - 1], s, shifted(i, r))
+        for r in range(1, n)
+    ]
+    for copy in dots_copies:
+        copy.start()
     terms_out[...] = terms[...].astype(jnp.bfloat16)
     terms_copies = [
         send(
@@ -362,15 +394,6 @@
     def _():
         terms_in[i] = terms_out[part(s), :]
 
-    dots[0] = jnp.broadcast_to(
-        jnp.sum(dot_fold[part(s), :], axis=1, keepdims=True), (rows, 128)
-    )
-    dots_copies = [
-        send(dots.at[0], dots.at[r], dots_send.at[r - 1], dots_recv.at[r - 1], s, shifted(i, r))
-        for r in range(1, n)
-    ]
-    for copy in dots_copies:
-        copy.start()
     for copy in dots_copies:
         copy.wait_recv()
     dot_sum = dots[0]
@@ -404,6 +427,11 @@
         own_copies[0].wait_send()
         terms_copies[0].wait_send()
 
+    @pl.when(near)
+    def _():
+        for copy in relays:
+            copy.wait_send()
+
     @pl.when(at_end)
     def _():
         for k in range(pieces):
@@ -414,6 +442,17 @@
         for k in range(pieces):
             second(k).wait_send()
             third(k, outer).wait_send()
+
+
+def hand_over(hidden_in, grad_in, hidden_out, grad_out, sem):
+    copies = [
+        pltpu.make_async_copy(hidden_in, hidden_out, sem.at[0]),
+        pltpu.make_async_copy(grad_in, grad_out, sem.at[1]),
+    ]
+    for copy in copies:
+        copy.start()
+    for copy in copies:
+        copy.wait()
 
 
 def line_body(item_last, adapter, user_gain, w_gate, w_up, owners, item_rows, lengths, d_hidden):
@@ -428,12 +467,13 @@
     sems = lambda count: pltpu.SemaphoreType.DMA((count,))
     pieces = width // 512 + width // 256
     sums = pltpu.VMEM((items, 3 * width), bf16)
-    return pl.pallas_call(
+    out_shape = (
+        jax.ShapeDtypeStruct((row_count, width), bf16),
+        jax.ShapeDtypeStruct((rows, own_width), f32),
+    )
+    results = pl.pallas_call(
         functools.partial(line_kernel, n),
-        out_shape=(
-            jax.ShapeDtypeStruct((row_count, width), bf16),
-            jax.ShapeDtypeStruct((rows, own_width), f32),
-        ),
+        out_shape=out_shape,
         in_specs=[vmem] * 5 + [anywhere] * 4,
         out_specs=(vmem, vmem),
         scratch_shapes=[
@@ -453,7 +493,7 @@
             pltpu.VMEM((items, depth), bf16),
             pltpu.VMEM((n, rows, own_width), bf16),
             sems(4),
-            sems(n), sems(n),
+            sems(2), sems(n), sems(n),
             sems(n - 1), sems(n - 1),
             sems(n - 1), sems(n - 1),
             sems(pieces), sems(pieces),
@@ -472,6 +512,14 @@
         owners.reshape(1, -1), item_rows.reshape(1, -1), lengths.reshape(1, -1),
         item_last, user_gain.reshape(1, -1), adapter, d_hidden, w_gate, w_up,
     )
+    return pl.pallas_call(
+        hand_over,
+        out_shape=out_shape,
+        in_specs=[anywhere] * 2,
+        out_specs=(anywhere, anywhere),
+        scratch_shapes=[sems(2)],
+        compiler_params=pltpu.CompilerParams(vmem_limit_bytes=60 * 1024 * 1024),
+    )(*results)
 
 
 def solution(mesh):

time: 66.3 us -> 77.4 us (1.17)
  Pallas kernels: 61.5 us -> 75.9 us
  local copies, waits for them, and re-layouts: 3.33 us -> 0 us
    pallas_call x1 -> x2, Pallas kernels: 61.5 us -> 75.9 us  [the longest x1 58.9 us: line_body(): pl.pallas_call(functools.partial(line_kernel, n), out_shape=out_shape, in...]
    unnamed x2 -> x0, local copies, waits for them, and re-layouts: 3.33 us -> none
where the time goes in v4:
time: 77.4 us; the launch traced here: 77.2 us
  Pallas kernels  75.9 us (98%)
  between operations  1.29 us (2%)
    pallas_call x1, Pallas kernels, line_body(): pl.pallas_call(functools.partial(line_kernel, n), out_shape=out_shape, in...  58.9 us
    pallas_call x1, Pallas kernels, line_body(): pl.pallas_call(hand_over, out_shape=out_shape, in_specs=[anywhere] * 2, o...  17 us

profile of v4, /device:TPU:0, one launch (start us, length us, event | category | flops | bytes accessed | tf_op | source)
XLA Modules:
  0.0 77.2 jit_solution(10258592720189918466)
XLA Ops:
  1.3 58.9 %shard_map.104 = (bf16[128,1536]{1,0:T(8,128)(2,1)}, f32[32,1024]{1,0:T(8,128)}) custom-call(s32[1,128]{1,0:T(1,128)} %bitcast.6, s32[1,128]{1,0:T(1,128)} %bitcast.7, s32[1,1]{1,0:T(1,128)} %bitcast.4.length_ref, bf16[32,2048]{1,0:T(8,128)(2,1)} %item_ref.1, f32[1,4096]{1,0:T(1,128)} %bitcast.5, bf16[2048,1024]{1,0:T(8,128)(2,1)} %adapter_hbm.1, ...), custom_call_target="tpu_custom_call" | custom-call | flops 1610612736 | bytes 6291456 | tf_op jit(solution)/shard_map/pallas_call | solution.py:474
  60.2 17.0 %shard_map.105 = (bf16[128,1536]{1,0:T(8,128)(2,1)}, f32[32,1024]{1,0:T(8,128)}) custom-call(bf16[128,1536]{1,0:T(8,128)(2,1)} %get-tuple-element.4.hidden_in, f32[32,1024]{1,0:T(8,128)} %get-tuple-element.5.grad_in), custom_call_target="tpu_custom_call" | custom-call | tf_op jit(solution)/shard_map/pallas_call | solution.py:515

commit v5 on v4

--- a/solution.py
+++ b/solution.py
@@ -444,15 +444,9 @@
             third(k, outer).wait_send()
 
 
-def hand_over(hidden_in, grad_in, hidden_out, grad_out, sem):
-    copies = [
-        pltpu.make_async_copy(hidden_in, hidden_out, sem.at[0]),
-        pltpu.make_async_copy(grad_in, grad_out, sem.at[1]),
-    ]
-    for copy in copies:
-        copy.start()
-    for copy in copies:
-        copy.wait()
+def hand_over(hidden_in, grad_in, hidden_out, grad_out):
+    hidden_out[...] = hidden_in[...]
+    grad_out[...] = grad_in[...]
 
 
 def line_body(item_last, adapter, user_gain, w_gate, w_up, owners, item_rows, lengths, d_hidden):
@@ -515,10 +509,8 @@
     return pl.pallas_call(
         hand_over,
         out_shape=out_shape,
-        in_specs=[anywhere] * 2,
-        out_specs=(anywhere, anywhere),
-        scratch_shapes=[sems(2)],
-        compiler_params=pltpu.CompilerParams(vmem_limit_bytes=60 * 1024 * 1024),
+        in_specs=[vmem] * 2,
+        out_specs=(vmem, vmem),
     )(*results)
 
 

time: 77.4 us -> 62.2 us (0.80)
  Pallas kernels: 75.9 us -> 60.8 us
    pallas_call x1, Pallas kernels: 17 us -> 1.83 us  [line_body(): pl.pallas_call(hand_over, out_shape=out_shape, in_specs=[vmem] * 2, out_s...]
where the time goes in v5:
time: 62.2 us; the launch traced here: 62 us
  Pallas kernels  60.8 us (98%)
  between operations  1.29 us (2%)
    pallas_call x1, Pallas kernels, line_body(): pl.pallas_call(functools.partial(line_kernel, n), out_shape=out_shape, in...  58.9 us
    pallas_call x1, Pallas kernels, line_body(): pl.pallas_call(hand_over, out_shape=out_shape, in_specs=[vmem] * 2, out_s...  1.83 us

profile of v5, /device:TPU:0, one launch (start us, length us, event | category | flops | bytes accessed | tf_op | source)
XLA Modules:
  0.0 62.0 jit_solution(6284669232120343685)
XLA Ops:
  1.3 58.9 %shard_map.104 = (bf16[128,1536]{1,0:T(8,128)(2,1)}, f32[32,1024]{1,0:T(8,128)}) custom-call(s32[1,128]{1,0:T(1,128)} %bitcast.6, s32[1,128]{1,0:T(1,128)} %bitcast.7, s32[1,1]{1,0:T(1,128)} %bitcast.4.length_ref, bf16[32,2048]{1,0:T(8,128)(2,1)} %item_ref.1, f32[1,4096]{1,0:T(1,128)} %bitcast.5, bf16[2048,1024]{1,0:T(8,128)(2,1)} %adapter_hbm.1, ...), custom_call_target="tpu_custom_call" | custom-call | flops 1610612736 | bytes 6291456 | tf_op jit(solution)/shard_map/pallas_call | solution.py:468
  60.2 1.8 %shard_map.105 = (bf16[128,1536]{1,0:T(8,128)(2,1)}, f32[32,1024]{1,0:T(8,128)}) custom-call(bf16[128,1536]{1,0:T(8,128)(2,1)} %get-tuple-element.4.hidden_in, f32[32,1024]{1,0:T(8,128)} %get-tuple-element.5.grad_in), custom_call_target="tpu_custom_call" | custom-call | tf_op jit(solution)/shard_map/pallas_call | solution.py:509
